TPU v7x, 32 devices: a whole 2x2x4 slice. The times are simulated.
32 devices in a mesh: dp: 4 (over x, core), fsdp: 8 (over z, y).
Axes of the slice: x: 2, y: 2, z: 4, core: 2. Of those that a mesh axis runs over, the one named last changes fastest.
Arguments:
- inputs: bfloat16 [2, 4096, 1536], P(None, ('dp', 'fsdp')), may hold values from -6 to 6
- documents: int32 [2, 32, 128], P(None, ('dp', 'fsdp')), may hold values from 0 to 1, never falling along the last dimension, each value on 1 to 96 neighbouring positions
- out_grad: bfloat16 [2, 4096, 1536], P(None, ('dp', 'fsdp')), may hold values from -6 to 6
- query_weight: bfloat16 [1536, 1536], P(('dp', 'fsdp')), may hold values from -0.15625 to 0.15625
- key_weight: bfloat16 [1536, 1536], P(('dp', 'fsdp')), may hold values from -0.15625 to 0.15625
- value_weight: bfloat16 [1536, 1536], P(('dp', 'fsdp')), may hold values from -0.15625 to 0.15625
- outgate_weight: bfloat16 [1536, 1536], P(('dp', 'fsdp')), may hold values from -0.15625 to 0.15625
- output_weight: bfloat16 [1536, 1536], P(('dp', 'fsdp')), may hold values from -0.4375 to 0.4375
- forget_weight: bfloat16 [1536, 24], P(('dp', 'fsdp')), may hold values from -0.15625 to 0.15625
- forget_bias: float32 [24], replicated, may hold values from 0 to 6
- gains: bfloat16 [1536, 4], P(('dp', 'fsdp')), may hold values from 0.5 to 1.5
- swiglu_gate: bfloat16 [1536, 4096], P(('dp', 'fsdp')), may hold values from -0.15625 to 0.15625
- swiglu_up: bfloat16 [1536, 4096], P(('dp', 'fsdp')), may hold values from -0.15625 to 0.15625
- swiglu_down: bfloat16 [4096, 1536], P(('dp', 'fsdp')), may hold values from -0.1875 to 0.1875
Outputs:
- outputs: bfloat16 [2, 4096, 1536], P(None, ('dp', 'fsdp'))
- input_grad: bfloat16 [2, 4096, 1536], P(None, ('dp', 'fsdp'))
- query_grad: float32 [1536, 1536], P(('dp', 'fsdp'))
- key_grad: float32 [1536, 1536], P(('dp', 'fsdp'))
- value_grad: float32 [1536, 1536], P(('dp', 'fsdp'))
- outgate_grad: float32 [1536, 1536], P(('dp', 'fsdp'))
- output_grad: float32 [1536, 1536], P(('dp', 'fsdp'))
- forget_grad: float32 [1536, 24], P(('dp', 'fsdp'))
- bias_grad: float32 [24], replicated
- gains_grad: float32 [1536, 4], P(('dp', 'fsdp'))
- gate_grad: float32 [1536, 4096], P(('dp', 'fsdp'))
- up_grad: float32 [1536, 4096], P(('dp', 'fsdp'))
- down_grad: float32 [4096, 1536], P(('dp', 'fsdp'))
Inputs may be any that keep to these rules, and one draw needn't show every extreme that they name: Along a device's tokens of one micro-batch the document number never falls; a document has 1 to 96 tokens there, so a device's block holds one or two documents.
All inputs are finite; a program needn't handle non-finite values.
Results may differ from a plain program's by a relative error of at most 0.015.
Values may be sent and summed in bfloat16 or wider, within the bound.
A program may use at most 256 MiB of HBM per device.

v0:
```python
import math

import jax
import jax.numpy as jnp
from jax import lax
from jax.sharding import PartitionSpec as P

EPSILON = 1e-06


def rms_scale(tensor):
    return lax.rsqrt(jnp.mean(tensor * tensor, axis=-1, keepdims=True) + EPSILON)


def norm_back(grad_normed, normed, scale):
    return scale * (grad_normed - normed * jnp.mean(grad_normed * normed, axis=-1, keepdims=True))


def product(left_side, right_side):
    return jnp.dot(left_side, right_side, preferred_element_type=jnp.float32)


def product_tn(left_side, right_side):
    return lax.dot_general(
        left_side, right_side, (((0,), (0,)), ((), ())), preferred_element_type=jnp.float32
    )


def product_nt(left_side, right_side):
    return lax.dot_general(
        left_side, right_side, (((1,), (1,)), ((), ())), preferred_element_type=jnp.float32
    )


def collect(query_w, key_w, value_w, ogate_w, output_w, forget_w, gain_cols, gate_w, up_w, down_w):
    return (
        lax.all_gather(query_w, ("dp", "fsdp"), axis=0, tiled=True),
        lax.all_gather(key_w, ("dp", "fsdp"), axis=0, tiled=True),
        lax.all_gather(value_w, ("dp", "fsdp"), axis=0, tiled=True),
        lax.all_gather(ogate_w, ("dp", "fsdp"), axis=0, tiled=True),
        lax.all_gather(output_w, ("dp", "fsdp"), axis=0, tiled=True),
        lax.all_gather(forget_w, ("dp", "fsdp"), axis=0, tiled=True),
        lax.all_gather(gain_cols, ("dp", "fsdp"), axis=0, tiled=True),
        lax.all_gather(gate_w, ("dp", "fsdp"), axis=0, tiled=True),
        lax.all_gather(up_w, ("dp", "fsdp"), axis=0, tiled=True),
        lax.all_gather(down_w, ("dp", "fsdp"), axis=0, tiled=True),
    )


def spread(query_g, key_g, value_g, ogate_g, output_g, forget_g, gain_g, gate_g, up_g, down_g):
    first = (
        lax.psum_scatter(query_g, ("dp", "fsdp"), scatter_dimension=0, tiled=True),
        lax.psum_scatter(key_g, ("dp", "fsdp"), scatter_dimension=0, tiled=True),
        lax.psum_scatter(value_g, ("dp", "fsdp"), scatter_dimension=0, tiled=True),
        lax.psum_scatter(ogate_g, ("dp", "fsdp"), scatter_dimension=0, tiled=True),
        lax.psum_scatter(forget_g, ("dp", "fsdp"), scatter_dimension=0, tiled=True),
        lax.psum_scatter(gain_g, ("dp", "fsdp"), scatter_dimension=0, tiled=True),
    )
    second = (
        lax.psum_scatter(output_g, ("dp", "fsdp"), scatter_dimension=0, tiled=True),
        lax.psum_scatter(gate_g, ("dp", "fsdp"), scatter_dimension=0, tiled=True),
    )
    third = lax.psum_scatter(up_g, ("dp", "fsdp"), scatter_dimension=0, tiled=True)
    fourth = lax.psum_scatter(down_g, ("dp", "fsdp"), scatter_dimension=0, tiled=True)
    return (
        first[0],
        first[1],
        first[2],
        first[3],
        second[0],
        first[4],
        first[5],
        second[1],
        third,
        fourth,
    )


def attention_scores(query_n, key_n, decay, allowed, score_root):
    scores = (
        jnp.einsum("ihd,jhd->hij", query_n, key_n, preferred_element_type=jnp.float32) / score_root
    )
    scores = scores + decay[:, :, None] - decay[:, None, :]
    return jnp.where(allowed[None], scores, -1e30)


def local(
    inputs,
    documents,
    out_grad,
    query_weight,
    key_weight,
    value_weight,
    outgate_weight,
    output_weight,
    forget_weight,
    forget_bias,
    gains,
    swiglu_gate,
    swiglu_up,
    swiglu_down,
):
    head_count = forget_weight.shape[1]
    micro_count = inputs.shape[0]
    row_count = inputs.shape[1]
    model_width = inputs.shape[2]
    head_width = model_width // head_count
    score_root = math.sqrt(head_width)
    positions = jnp.arange(row_count)
    results = []
    row_grads = []
    totals = None
    bias_local = jnp.zeros((head_count,), jnp.float32)
    for micro_step in range(micro_count):
        weights = collect(
            query_weight,
            key_weight,
            value_weight,
            outgate_weight,
            output_weight,
            forget_weight,
            gains,
            swiglu_gate,
            swiglu_up,
            swiglu_down,
        )
        query_w, key_w, value_w, ogate_w, output_w, forget_w, gain_all, gate_w, up_w, down_w = (
            weights
        )
        gain_cols = gain_all.astype(jnp.float32)
        row_block = inputs[micro_step].astype(jnp.float32)
        doc_ids = documents[micro_step, 0]
        upstream = out_grad[micro_step].astype(jnp.float32)
        allowed = (doc_ids[:, None] == doc_ids[None, :]) & (
            positions[None, :] <= positions[:, None]
        )
        scale_one = rms_scale(row_block)
        normed_one = row_block * scale_one
        hidden_one = (normed_one * gain_cols[:, 0]).astype(jnp.bfloat16)
        queries = product(hidden_one, query_w).reshape(row_count, head_count, head_width)
        keys_raw = product(hidden_one, key_w).reshape(row_count, head_count, head_width)
        values_low = (
            product(hidden_one, value_w)
            .astype(jnp.bfloat16)
            .reshape(row_count, head_count, head_width)
        )
        gate_pre = product(hidden_one, ogate_w)
        forget_pre = product(hidden_one, forget_w) + forget_bias
        query_gain = gain_cols[:, 1].reshape(head_count, head_width)
        key_gain = gain_cols[:, 2].reshape(head_count, head_width)
        query_scale = rms_scale(queries)
        query_hat = queries * query_scale
        query_n = (query_hat * query_gain).astype(jnp.bfloat16)
        key_scale = rms_scale(keys_raw)
        key_hat = keys_raw * key_scale
        key_n = (key_hat * key_gain).astype(jnp.bfloat16)
        decay = jnp.cumsum(jax.nn.log_sigmoid(forget_pre), axis=0).T
        scores = attention_scores(query_n, key_n, decay, allowed, score_root)
        row_max = jnp.max(scores, axis=-1, keepdims=True)
        shifted = jnp.exp(scores - row_max)
        row_total = jnp.sum(shifted, axis=-1, keepdims=True)
        log_total = row_max + jnp.log(row_total)
        probs_low = (shifted / row_total).astype(jnp.bfloat16)
        attended = jnp.einsum(
            "hij,jhd->ihd", probs_low, values_low, preferred_element_type=jnp.float32
        ).reshape(row_count, model_width)
        gate_sig = jax.nn.sigmoid(gate_pre)
        gated = (attended * gate_sig).astype(jnp.bfloat16)
        middle = row_block + product(gated, output_w)
        scale_two = rms_scale(middle)
        normed_two = middle * scale_two
        hidden_two = (normed_two * gain_cols[:, 3]).astype(jnp.bfloat16)
        gate_act = product(hidden_two, gate_w)
        up_act = product(hidden_two, up_w)
        gate_sg = jax.nn.sigmoid(gate_act)
        activated = (gate_act * gate_sg * up_act).astype(jnp.bfloat16)
        results.append((middle + product(activated, down_w)).astype(jnp.bfloat16))
        weights = collect(
            query_weight,
            key_weight,
            value_weight,
            outgate_weight,
            output_weight,
            forget_weight,
            gains,
            swiglu_gate,
            swiglu_up,
            swiglu_down,
        )
        query_w, key_w, value_w, ogate_w, output_w, forget_w, gain_all, gate_w, up_w, down_w = (
            weights
        )
        down_in = upstream.astype(jnp.bfloat16)
        grad_down = product_tn(activated, down_in)
        grad_act = product_nt(down_in, down_w)
        grad_gate = (grad_act * up_act * gate_sg * (1.0 + gate_act * (1.0 - gate_sg))).astype(
            jnp.bfloat16
        )
        grad_upact = (grad_act * gate_act * gate_sg).astype(jnp.bfloat16)
        grad_gatew = product_tn(hidden_two, grad_gate)
        grad_upw = product_tn(hidden_two, grad_upact)
        grad_hidden_two = product_nt(grad_gate, gate_w) + product_nt(grad_upact, up_w)
        grad_gain_three = jnp.sum(grad_hidden_two * normed_two, axis=0)
        grad_middle = upstream + norm_back(grad_hidden_two * gain_cols[:, 3], normed_two, scale_two)
        output_in = grad_middle.astype(jnp.bfloat16)
        grad_outw = product_tn(gated, output_in)
        grad_gated = product_nt(output_in, output_w)
        grad_attended = (
            (grad_gated * gate_sig).astype(jnp.bfloat16).reshape(row_count, head_count, head_width)
        )
        grad_gatepre = (grad_gated * attended * gate_sig * (1.0 - gate_sig)).astype(jnp.bfloat16)
        grad_ogatew = product_tn(hidden_one, grad_gatepre)
        scores_again = attention_scores(query_n, key_n, decay, allowed, score_root)
        probs = jnp.exp(scores_again - log_total)
        grad_probs = jnp.einsum(
            "ihd,jhd->hij", grad_attended, values_low, preferred_element_type=jnp.float32
        )
        grad_values = jnp.einsum(
            "hij,ihd->jhd",
            probs.astype(jnp.bfloat16),
            grad_attended,
            preferred_element_type=jnp.float32,
        )
        grad_scores = (
            probs * (grad_probs - jnp.sum(probs * grad_probs, axis=-1, keepdims=True))
        ).astype(jnp.bfloat16)
        grad_query_n = (
            jnp.einsum("hij,jhd->ihd", grad_scores, key_n, preferred_element_type=jnp.float32)
            / score_root
        )
        grad_key_n = (
            jnp.einsum("hij,ihd->jhd", grad_scores, query_n, preferred_element_type=jnp.float32)
            / score_root
        )
        scores_wide = grad_scores.astype(jnp.float32)
        grad_decay = (jnp.sum(scores_wide, axis=2) - jnp.sum(scores_wide, axis=1)).T
        grad_logf = jnp.flip(jnp.cumsum(jnp.flip(grad_decay, 0), axis=0), 0)
        grad_forget = (grad_logf * (1.0 - jax.nn.sigmoid(forget_pre))).astype(jnp.bfloat16)
        bias_local = bias_local + jnp.sum(grad_forget.astype(jnp.float32), axis=0)
        grad_forgetw = product_tn(hidden_one, grad_forget)
        grad_gain_query = jnp.sum(grad_query_n * query_hat, axis=0).reshape(model_width)
        grad_query = (
            norm_back(grad_query_n * query_gain, query_hat, query_scale)
            .astype(jnp.bfloat16)
            .reshape(row_count, model_width)
        )
        grad_gain_key = jnp.sum(grad_key_n * key_hat, axis=0).reshape(model_width)
        grad_key = (
            norm_back(grad_key_n * key_gain, key_hat, key_scale)
            .astype(jnp.bfloat16)
            .reshape(row_count, model_width)
        )
        grad_value = grad_values.astype(jnp.bfloat16).reshape(row_count, model_width)
        grad_queryw = product_tn(hidden_one, grad_query)
        grad_keyw = product_tn(hidden_one, grad_key)
        grad_valuew = product_tn(hidden_one, grad_value)
        grad_hidden_one = (
            product_nt(grad_query, query_w)
            + product_nt(grad_key, key_w)
            + product_nt(grad_value, value_w)
            + product_nt(grad_gatepre, ogate_w)
            + product_nt(grad_forget, forget_w)
        )
        grad_gain_one = jnp.sum(grad_hidden_one * normed_one, axis=0)
        grad_rows = grad_middle + norm_back(
            grad_hidden_one * gain_cols[:, 0], normed_one, scale_one
        )
        row_grads.append(grad_rows.astype(jnp.bfloat16))
        grad_gains = jnp.stack(
            [grad_gain_one, grad_gain_query, grad_gain_key, grad_gain_three], axis=1
        )
        terms = (
            grad_queryw,
            grad_keyw,
            grad_valuew,
            grad_ogatew,
            grad_outw,
            grad_forgetw,
            grad_gains,
            grad_gatew,
            grad_upw,
            grad_down,
        )
        shares = spread(*terms)
        if micro_step == 0:
            totals = tuple(shares)
        else:
            totals = tuple((previous + current for previous, current in zip(totals, shares)))
    bias_sum = lax.psum(bias_local, ("dp", "fsdp"))
    return (
        jnp.stack(results, axis=0),
        jnp.stack(row_grads, axis=0),
        totals[0],
        totals[1],
        totals[2],
        totals[3],
        totals[4],
        totals[5],
        bias_sum,
        totals[6],
        totals[7],
        totals[8],
        totals[9],
    )


def solution(mesh):
    in_specs = (
        P(None, ("dp", "fsdp"), None),
        P(None, ("dp", "fsdp"), None),
        P(None, ("dp", "fsdp"), None),
        P(("dp", "fsdp"), None),
        P(("dp", "fsdp"), None),
        P(("dp", "fsdp"), None),
        P(("dp", "fsdp"), None),
        P(("dp", "fsdp"), None),
        P(("dp", "fsdp"), None),
        P(),
        P(("dp", "fsdp"), None),
        P(("dp", "fsdp"), None),
        P(("dp", "fsdp"), None),
        P(("dp", "fsdp"), None),
    )
    out_specs = (
        P(None, ("dp", "fsdp"), None),
        P(None, ("dp", "fsdp"), None),
        P(("dp", "fsdp"), None),
        P(("dp", "fsdp"), None),
        P(("dp", "fsdp"), None),
        P(("dp", "fsdp"), None),
        P(("dp", "fsdp"), None),
        P(("dp", "fsdp"), None),
        P(),
        P(("dp", "fsdp"), None),
        P(("dp", "fsdp"), None),
        P(("dp", "fsdp"), None),
        P(("dp", "fsdp"), None),
    )
    return jax.shard_map(local, mesh=mesh, in_specs=in_specs, out_specs=out_specs, check_vma=False)
```

profile of v0, /device:TPU:0, one launch (start us, length us, event | category | flops | bytes accessed | tf_op | source)
XLA Modules:
  0.0 2450.1 jit_solution(15846026412050133962)
XLA Ops:
  12.7 70.1 %all-gather = bf16[32,48,4]{1,2,0:T(4,128)(2,1)S(1)} all-gather(bf16[1,48,4]{1,2,0:T(4,128)(2,1)} %bitcast.373), channel_id=1, replica_groups=mesh['dp'=4,'fsdp'=8] {'dp','fsdp'}, dimensions={0}, use_global_device_ids=true | all-gather | bytes 12672 | tf_op jit(solution)/shard_map/all_gather | solution.py:43
  83.0 65.3 %all-gather.1 = bf16[32,48,24]{1,2,0:T(8,128)(2,1)S(1)} all-gather(bf16[1,48,24]{1,2,0:T(8,128)(2,1)} %bitcast.372), channel_id=1, replica_groups=mesh['dp'=4,'fsdp'=8] {'dp','fsdp'}, dimensions={0}, use_global_device_ids=true | all-gather | bytes 76032 | tf_op jit(solution)/shard_map/all_gather | solution.py:42
  165.2 43.7 %all-gather.13.cloned.1.call-done = bf16[1536,1536]{1,0:T(8,128)(2,1)} async-done(((bf16[48,1536]{1,0:T(8,128)(2,1)}), bf16[1536,1536]{1,0:T(8,128)(2,1)}) %all-gather.13.cloned.1.call-update) | async-done | bytes 4718608 | tf_op jit(solution)/shard_map/all_gather | solution.py:37
  240.1 34.1 %all-gather.17.cloned.1.call-done = bf16[1536,1536]{1,0:T(8,128)(2,1)} async-done(((bf16[48,1536]{1,0:T(8,128)(2,1)}), bf16[1536,1536]{1,0:T(8,128)(2,1)}) %all-gather.17.cloned.1.call-update) | async-done | bytes 4718608 | tf_op jit(solution)/shard_map/all_gather | solution.py:40
  278.4 61.1 %all-gather.19.cloned.1.call-done = bf16[1536,1536]{1,0:T(8,128)(2,1)} async-done(((bf16[48,1536]{1,0:T(8,128)(2,1)}), bf16[1536,1536]{1,0:T(8,128)(2,1)}) %all-gather.19.cloned.1.call-update) | async-done | bytes 4718608 | tf_op jit(solution)/shard_map/all_gather | solution.py:41
  349.3 87.8 %all-gather.21.cloned.1.call-done = bf16[1536,4096]{1,0:T(8,128)(2,1)} async-done(((bf16[48,4096]{1,0:T(8,128)(2,1)}), bf16[1536,4096]{1,0:T(8,128)(2,1)}) %all-gather.21.cloned.1.call-update) | async-done | bytes 12582928 | tf_op jit(solution)/shard_map/all_gather | solution.py:44
  443.7 90.6 %all-gather.23.cloned.1.call-done = bf16[1536,4096]{1,0:T(8,128)(2,1)} async-done(((bf16[48,4096]{1,0:T(8,128)(2,1)}), bf16[1536,4096]{1,0:T(8,128)(2,1)}) %all-gather.23.cloned.1.call-update) | async-done | bytes 12582928 | tf_op jit(solution)/shard_map/all_gather | solution.py:45
  542.0 89.5 %all-gather.25.cloned.1.call-done = bf16[4096,1536]{1,0:T(8,128)(2,1)} async-done(((bf16[128,1536]{1,0:T(8,128)(2,1)}), bf16[4096,1536]{1,0:T(8,128)(2,1)}) %all-gather.25.cloned.1.call-update) | async-done | bytes 12582928 | tf_op jit(solution)/shard_map/all_gather | solution.py:46
  652.4 11.4 multiply_reduce_fusion.3
  827.2 11.5 fusion.147
  838.7 16.5 convolution_add_fusion.2
  855.3 11.5 fusion.148
  866.8 16.5 convolution_add_fusion.1
  884.4 11.6 fusion.75
  896.1 17.4 convolution_add_fusion
  914.1 38.7 %psum.7 = f32[24]{0:T(128)} all-reduce(f32[24]{0:T(128)S(1)} %add.330), channel_id=1, replica_groups=mesh['dp'=4,'fsdp'=8] {'dp','fsdp'}, use_global_device_ids=true, to_apply=%region_44.45 | all-reduce | flops 24 | bytes 192 | tf_op jit(solution)/shard_map/psum | solution.py:289
  980.3 139.7 %reduce-scatter.15.cloned.1.call-done = f32[48,1536]{1,0:T(8,128)} async-done(((f32[1536,1536]{1,0:T(8,128)}), f32[48,1536]{1,0:T(8,128)}) %reduce-scatter.15.cloned.1.call-update) | async-done | bytes 294928 | tf_op jit(solution)/shard_map/reduce_scatter | solution.py:52
  1119.9 142.0 %reduce-scatter.17.cloned.1.call-done = f32[48,1536]{1,0:T(8,128)} async-done(((f32[1536,1536]{1,0:T(8,128)}), f32[48,1536]{1,0:T(8,128)}) %reduce-scatter.17.cloned.1.call-update) | async-done | bytes 294928 | tf_op jit(solution)/shard_map/reduce_scatter | solution.py:53
  1261.9 141.2 %reduce-scatter.19.cloned.1.call-done = f32[48,1536]{1,0:T(8,128)} async-done(((f32[1536,1536]{1,0:T(8,128)}), f32[48,1536]{1,0:T(8,128)}) %reduce-scatter.19.cloned.1.call-update) | async-done | bytes 294928 | tf_op jit(solution)/shard_map/reduce_scatter | solution.py:54
  1403.1 141.8 %reduce-scatter.21.cloned.1.call-done = f32[48,1536]{1,0:T(8,128)} async-done(((f32[1536,1536]{1,0:T(8,128)}), f32[48,1536]{1,0:T(8,128)}) %reduce-scatter.21.cloned.1.call-update) | async-done | bytes 294928 | tf_op jit(solution)/shard_map/reduce_scatter | solution.py:55
  1544.9 141.0 %reduce-scatter.23.cloned.1.call-done = f32[48,1536]{1,0:T(8,128)} async-done(((f32[1536,1536]{1,0:T(8,128)}), f32[48,1536]{1,0:T(8,128)}) %reduce-scatter.23.cloned.1.call-update) | async-done | bytes 294928 | tf_op jit(solution)/shard_map/reduce_scatter | solution.py:60
  1685.9 252.2 %reduce-scatter.25.cloned.1.call-done = f32[48,4096]{1,0:T(8,128)} async-done(((f32[1536,4096]{1,0:T(8,128)}), f32[48,4096]{1,0:T(8,128)}) %reduce-scatter.25.cloned.1.call-update) | async-done | bytes 786448 | tf_op jit(solution)/shard_map/reduce_scatter | solution.py:61
  1938.1 251.9 %reduce-scatter.27.cloned.1.call-done = f32[48,4096]{1,0:T(8,128)} async-done(((f32[1536,4096]{1,0:T(8,128)}), f32[48,4096]{1,0:T(8,128)}) %reduce-scatter.27.cloned.1.call-update) | async-done | bytes 786448 | tf_op jit(solution)/shard_map/reduce_scatter | solution.py:63
  2190.0 253.0 %reduce-scatter.29.cloned.1.call-done = f32[128,1536]{1,0:T(8,128)} async-done(((f32[4096,1536]{1,0:T(8,128)}), f32[128,1536]{1,0:T(8,128)}) %reduce-scatter.29.cloned.1.call-update) | async-done | bytes 786448 | tf_op jit(solution)/shard_map/reduce_scatter | solution.py:64
  (430 shorter events, 293.9 us)
Async XLA Ops:
  7.2 145.2 %copy-start = (bf16[2,128,1536]{2,1,0:T(8,128)(2,1)S(1)}, bf16[2,128,1536]{2,1,0:T(8,128)(2,1)}, u32[]{:S(2)}) copy-start(bf16[2,128,1536]{2,1,0:T(8,128)(2,1)} %param.14) | copy-start | bytes 2359300
  7.2 145.2 %copy-start.103 = (f32[24]{0:T(128)S(1)}, f32[24]{0:T(128)}, u32[]{:S(2)}) copy-start(f32[24]{0:T(128)} %param.23) | copy-start | bytes 292
  7.2 146.4 %copy-start.99 = (s32[2,1,128]{2,1,0:T(1,128)S(1)}, s32[2,1,128]{2,1,0:T(1,128)}, u32[]{:S(2)}) copy-start(s32[2,1,128]{2,1,0:T(1,128)} %param.15) | copy-start | bytes 3076
  7.2 147.8 %all-gather.11.cloned.1.call-start = ((), (), s32[]{:S(2)}) async-start(), calls=%async_computation.10 | async-start | bytes 4866048 | tf_op jit(solution)/shard_map/all_gather | solution.py:39
  7.9 150.5 %all-gather.15.cloned.1.call-start = ((), (), s32[]{:S(2)}) async-start(), calls=%async_computation.12 | async-start | bytes 4866048 | tf_op jit(solution)/shard_map/all_gather | solution.py:38
  8.7 200.2 %all-gather.13.cloned.1.call-start = ((), (), s32[]{:S(2)}) async-start(), calls=%async_computation.11 | async-start | bytes 4866048 | tf_op jit(solution)/shard_map/all_gather | solution.py:37
  9.4 264.8 %all-gather.17.cloned.1.call-start = ((), (), s32[]{:S(2)}) async-start(), calls=%async_computation.13 | async-start | bytes 4866048 | tf_op jit(solution)/shard_map/all_gather | solution.py:40
  10.0 329.5 %all-gather.19.cloned.1.call-start = ((), (), s32[]{:S(2)}) async-start(), calls=%async_computation.14 | async-start | bytes 4866048 | tf_op jit(solution)/shard_map/all_gather | solution.py:41
  10.6 426.5 %all-gather.21.cloned.1.call-start = ((), (), s32[]{:S(2)}) async-start(), calls=%async_computation.15 | async-start | bytes 12976128 | tf_op jit(solution)/shard_map/all_gather | solution.py:44
  11.2 523.1 %all-gather.23.cloned.1.call-start = ((), (), s32[]{:S(2)}) async-start(), calls=%async_computation.16 | async-start | bytes 12976128 | tf_op jit(solution)/shard_map/all_gather | solution.py:45
  11.9 619.5 %all-gather.25.cloned.1.call-start = ((), (), s32[]{:S(2)}) async-start(), calls=%async_computation.17 | async-start | bytes 12976128 | tf_op jit(solution)/shard_map/all_gather | solution.py:46
  12.7 956.0 %reduce-scatter.33.cloned.1.call-start = ((), (), s32[]{:S(2)}) async-start(), calls=%async_computation.27 | async-start | bytes 811008
  150.0 192.9 %copy-start.86 = (f32[128]{0:T(128)}, f32[128]{0:T(128)S(1)}, u32[]{:S(2)}) copy-start(f32[128]{0:T(128)S(1)} %get-tuple-element.101) | copy-start | bytes 1540
  349.2 185.0 %copy-start.13 = (bf16[128,1536]{1,0:T(8,128)(2,1)}, bf16[128,1536]{1,0:T(8,128)(2,1)S(1)}, u32[]{:S(2)}) copy-start(bf16[128,1536]{1,0:T(8,128)(2,1)S(1)} %multiply_convert_fusion.16) | copy-start | bytes 1179652
  443.7 187.8 %copy-start.42 = (bf16[2,128,1536]{2,1,0:T(8,128)(2,1)S(1)}, bf16[2,128,1536]{2,1,0:T(8,128)(2,1)}, u32[]{:S(2)}) copy-start(bf16[2,128,1536]{2,1,0:T(8,128)(2,1)} %param.16) | copy-start | bytes 2359300
  785.4 193.4 %reduce-scatter.31.cloned.1.call-start = ((), (), s32[]{:S(2)}) async-start(), calls=%async_computation.26 | async-start | bytes 811008
  789.7 330.3 %reduce-scatter.15.cloned.1.call-start = ((), (), s32[]{:S(2)}) async-start(), calls=%async_computation.18 | async-start | bytes 9732096 | tf_op jit(solution)/shard_map/reduce_scatter | solution.py:52
  798.7 463.3 %reduce-scatter.17.cloned.1.call-start = ((), (), s32[]{:S(2)}) async-start(), calls=%async_computation.19 | async-start | bytes 9732096 | tf_op jit(solution)/shard_map/reduce_scatter | solution.py:53
  805.3 597.8 %reduce-scatter.19.cloned.1.call-start = ((), (), s32[]{:S(2)}) async-start(), calls=%async_computation.20 | async-start | bytes 9732096 | tf_op jit(solution)/shard_map/reduce_scatter | solution.py:54
  811.9 733.0 %reduce-scatter.21.cloned.1.call-start = ((), (), s32[]{:S(2)}) async-start(), calls=%async_computation.21 | async-start | bytes 9732096 | tf_op jit(solution)/shard_map/reduce_scatter | solution.py:55
  818.7 867.2 %reduce-scatter.23.cloned.1.call-start = ((), (), s32[]{:S(2)}) async-start(), calls=%async_computation.22 | async-start | bytes 9732096 | tf_op jit(solution)/shard_map/reduce_scatter | solution.py:60
  826.3 1111.8 %reduce-scatter.25.cloned.1.call-start = ((), (), s32[]{:S(2)}) async-start(), calls=%async_computation.23 | async-start | bytes 25952256 | tf_op jit(solution)/shard_map/reduce_scatter | solution.py:61
  855.3 1334.7 %reduce-scatter.27.cloned.1.call-start = ((), (), s32[]{:S(2)}) async-start(), calls=%async_computation.24 | async-start | bytes 25952256 | tf_op jit(solution)/shard_map/reduce_scatter | solution.py:63
  883.3 1559.7 %reduce-scatter.29.cloned.1.call-start = ((), (), s32[]{:S(2)}) async-start(), calls=%async_computation.25 | async-start | bytes 25952256 | tf_op jit(solution)/shard_map/reduce_scatter | solution.py:64
  (115 other events, 1387.7 us)
Sparse Core Ops, SparseCore 0:
  11.0 66.3 all-gather.10
  80.3 62.9 all-gather.14
  146.2 62.6 all-gather.12
  211.7 62.4 all-gather.16
  277.0 62.4 all-gather.18
  342.2 94.8 all-gather.20
  440.0 94.2 all-gather.22
  537.2 94.2 all-gather.24
  785.6 93.6 reduce-scatter.32
  884.2 94.5 reduce-scatter.30
  985.3 134.5 reduce-scatter.14
  1127.3 134.5 reduce-scatter.16
  1268.4 134.6 reduce-scatter.18
  1410.4 134.4 reduce-scatter.20
  1551.2 134.5 reduce-scatter.22
  1693.9 244.1 reduce-scatter.24
  1944.9 244.9 reduce-scatter.26
  2198.0 245.0 reduce-scatter.28
where the time goes:
time: 2460 us; the launch traced here: 2450 us
  waiting for transfers between devices  1880 us (76%)
  matrix products  313 us (13%)
  blocking collectives  174 us (7%)
  local copies, waits for them, and re-layouts  42 us (2%)
    reduce_scatter x1, waiting for transfers between devices, spread(): lax.psum_scatter(down_g, ('dp', 'fsdp'), scatter_dimension=0, tiled=True)  253 us
    reduce_scatter x1, waiting for transfers between devices, spread(): lax.psum_scatter(gate_g, ('dp', 'fsdp'), scatter_dimension=0, tiled=True)  252 us
    reduce_scatter x1, waiting for transfers between devices, spread(): lax.psum_scatter(up_g, ('dp', 'fsdp'), scatter_dimension=0, tiled=True)  252 us
    reduce_scatter x1, waiting for transfers between devices, spread(): lax.psum_scatter(key_g, ('dp', 'fsdp'), scatter_dimension=0, tiled=True)  142 us
    reduce_scatter x1, waiting for transfers between devices, spread(): lax.psum_scatter(ogate_g, ('dp', 'fsdp'), scatter_dimension=0, tiled=True)  142 us
    reduce_scatter x1, waiting for transfers between devices, spread(): lax.psum_scatter(value_g, ('dp', 'fsdp'), scatter_dimension=0, tiled=True)  141 us
    reduce_scatter x1, waiting for transfers between devices, spread(): lax.psum_scatter(output_g, ('dp', 'fsdp'), scatter_dimension=0, tiled=True)  141 us
    reduce_scatter x1, waiting for transfers between devices, spread(): lax.psum_scatter(query_g, ('dp', 'fsdp'), scatter_dimension=0, tiled=True)  140 us
  transfers between devices with their start and end apart: 18, of which 15 were waited for; matrix products, arithmetic and copies ran while one was open for 9% of the time, Pallas kernels for 0%

commit v1 on v0

v1 whole, which is shorter than its diff:
```python
import math

import jax
import jax.numpy as jnp
import numpy as np
from jax import lax
from jax.sharding import PartitionSpec as P

EPSILON = 1e-06
BOTH = ("dp", "fsdp")
F32 = jnp.float32
BF16 = jnp.bfloat16


def rms_scale(tensor):
    return lax.rsqrt(jnp.mean(tensor * tensor, axis=-1, keepdims=True) + EPSILON)


def norm_back(grad_normed, normed, scale):
    return scale * (grad_normed - normed * jnp.mean(grad_normed * normed, axis=-1, keepdims=True))


def product(left_side, right_side):
    return jnp.dot(left_side, right_side, preferred_element_type=F32)


def product_tn(left_side, right_side):
    return lax.dot_general(
        left_side, right_side, (((0,), (0,)), ((), ())), preferred_element_type=F32
    )


def product_nt(left_side, right_side):
    return lax.dot_general(
        left_side, right_side, (((1,), (1,)), ((), ())), preferred_element_type=F32
    )


class Place:
    def __init__(self, mesh):
        self.dp = mesh.shape["dp"]
        self.fsdp = mesh.shape["fsdp"]
        self.zs = self.fsdp // 2
        self.core = self.perm(lambda x, c, z, y: (x, 1 - c, z, y))
        self.over_x = self.perm(lambda x, c, z, y: (1 - x, c, z, y))
        self.over_y = self.perm(lambda x, c, z, y: (x, c, z, 1 - y))
        self.over_xc = self.perm(lambda x, c, z, y: (1 - x, 1 - c, z, y))
        self.over_yc = self.perm(lambda x, c, z, y: (x, 1 - c, z, 1 - y))
        self.swap_xy = self.perm(lambda x, c, z, y: (y, c, z, x))
        order = []
        for z in range(self.zs):
            offs = sorted((j - z for j in range(self.zs)), key=lambda o: (abs(o), o if z % 2 else -o))
            order.append(offs)
        self.slots = [[order[z][t] for z in range(self.zs)] for t in range(self.zs)]

    def index(self, x, c, z, y):
        return (x * 2 + c) * self.fsdp + z * 2 + y

    def perm(self, target):
        pairs = []
        for x in range(2):
            for c in range(2):
                for z in range(self.zs):
                    for y in range(2):
                        to = target(x, c, z, y)
                        if to is not None:
                            pairs.append((self.index(x, c, z, y), self.index(*to)))
        return pairs

    def along(self, sign, hops):
        def target(x, c, z, y):
            back, to = z - sign * (hops - 1), z + sign
            if 0 <= back < self.zs and 0 <= to < self.zs:
                return (x, c, to, y)
            return None

        return self.perm(target)

    def toward(self, sign, offset):
        def target(x, c, z, y):
            if 0 <= z + sign * offset < self.zs:
                return (x, c, z + sign, y)
            return None

        return self.perm(target)


def send(value, perm):
    return lax.ppermute(value, BOTH, perm)


def pick(which, options):
    first = options[0]
    if all(option is first for option in options):
        return first
    return lax.select_n(which, *options)


def local(
    place,
    inputs,
    documents,
    out_grad,
    query_weight,
    key_weight,
    value_weight,
    outgate_weight,
    output_weight,
    forget_weight,
    forget_bias,
    gains,
    swiglu_gate,
    swiglu_up,
    swiglu_down,
):
    head_total = forget_weight.shape[1]
    micro_count, row_count, width = inputs.shape
    head_width = width // head_total
    heads = head_total // 4
    own_rows = query_weight.shape[0]
    part = width // 4
    hidden = swiglu_gate.shape[1] // 4
    zs = place.zs
    score_root = math.sqrt(head_width)
    positions = jnp.arange(row_count)

    dp_at = lax.axis_index("dp")
    fsdp_at = lax.axis_index("fsdp")
    x_at, c_at = dp_at // 2, dp_at % 2
    z_at, y_at = fsdp_at // 2, fsdp_at % 2
    at_y = y_at * 2 + c_at
    at_x = x_at * 2 + c_at

    def group_gather(value, across):
        there = send(value, across)
        return [value, there, send(value, place.core), send(there, place.core)]

    def group_sum(parts, across):
        core_own = send(parts[2].astype(BF16), place.core).astype(F32)
        core_across = send(parts[3].astype(BF16), place.core).astype(F32)
        over = send((parts[1] + core_across).astype(BF16), across).astype(F32)
        return parts[0] + core_own + over

    def exchange(blocks, at, perms):
        kept = [blocks(at ^ rel) for rel in range(4)]
        came = [kept[0]] + [send(kept[rel], perms[rel]) for rel in (1, 2, 3)]
        return [pick(at, [came[member ^ own] for own in range(4)]) for member in range(4)]

    y_perms = (None, place.core, place.over_y, place.over_yc)
    x_perms = (None, place.core, place.over_x, place.over_xc)

    def unit_gather(unit, across, across_at):
        near = {0: unit}
        right = left = unit
        for step in range(1, zs):
            right = send(right, place.along(1, step))
            left = send(left, place.along(-1, step))
            near[-step], near[step] = right, left
        crossed = []
        for slot in range(zs):
            chosen = pick(z_at, [near[place.slots[slot][z]] for z in range(zs)])
            crossed.append(send(chosen, across))
        rows = []
        for owner in range(zs):
            own = pick(z_at, [near[owner - z] for z in range(zs)])
            over = pick(
                z_at,
                [crossed[[place.slots[s][z] for s in range(zs)].index(owner - z)] for z in range(zs)],
            )
            rows.append([jnp.where(across_at == 0, own, over), jnp.where(across_at == 0, over, own)])
        return rows

    def unit_sum(blocks, across, across_at):
        summed = [None] * zs
        mine = lax.dynamic_index_in_dim(blocks, across_at, 1, keepdims=False)
        other = lax.dynamic_index_in_dim(blocks, 1 - across_at, 1, keepdims=False)
        for slot in reversed(range(zs)):
            owner = z_at + jnp.asarray(np.array(place.slots[slot], np.int32))[z_at]
            gone = lax.dynamic_index_in_dim(other, owner, 0, keepdims=False).astype(BF16)
            came = send(gone, across).astype(F32)
            summed[slot] = came + lax.dynamic_index_in_dim(mine, owner, 0, keepdims=False).astype(F32)

        def at_offset(offset):
            options = []
            for z in range(zs):
                offs = [place.slots[s][z] for s in range(zs)]
                options.append(summed[offs.index(offset)] if offset in offs else summed[0])
            return pick(z_at, options)

        total = summed[0]
        for sign in (1, -1):
            carried = None
            for offset in range(zs - 1, 0, -1):
                term = at_offset(sign * offset)
                if carried is not None:
                    term = term + carried
                carried = send(term.astype(BF16), place.toward(sign, offset)).astype(F32)
            total = total + carried
        return total

    small = lax.all_gather(
        jnp.concatenate([forget_weight, gains], axis=1), BOTH, axis=0, tiled=True
    )
    docs_all = [d[:, 0] for d in group_gather(documents, place.over_y)]
    rows_y = group_gather(inputs, place.over_y)

    attn_blocks = jnp.concatenate(
        [w.reshape(own_rows, 4, part) for w in (query_weight, key_weight, value_weight, outgate_weight)],
        axis=2,
    )
    attn_unit = jnp.stack(
        exchange(
            lambda j: lax.dynamic_index_in_dim(attn_blocks, j, 1, keepdims=False), at_y, y_perms
        )
    )
    attn_all = unit_gather(attn_unit, place.over_x, x_at)
    out_unit = send(output_weight, place.swap_xy)
    out_all = unit_gather(out_unit, place.over_x, x_at)
    ffn_blocks = jnp.concatenate(
        [w.reshape(own_rows, 4, hidden) for w in (swiglu_gate, swiglu_up)], axis=2
    )
    ffn_unit = jnp.stack(
        exchange(
            lambda j: lax.dynamic_index_in_dim(ffn_blocks, j, 1, keepdims=False), at_x, x_perms
        )
    )
    ffn_all = unit_gather(ffn_unit, place.over_y, y_at)
    down_all = unit_gather(swiglu_down, place.over_y, y_at)
    dy_x = group_gather(out_grad, place.over_x)

    def rows_from(units, first, columns):
        stacked = jnp.stack([jnp.stack(u) for u in units]).reshape(zs, 2, 2, 2, own_rows, columns)
        return stacked

    attn_w = (
        rows_from(attn_all, 0, 4 * part).transpose(1, 3, 0, 2, 4, 5).reshape(width, 4 * part)
    )
    ffn_w = (
        rows_from(ffn_all, 0, 2 * hidden).transpose(2, 3, 0, 1, 4, 5).reshape(width, 2 * hidden)
    )
    out_w = jnp.concatenate([v for u in out_all for v in u], axis=0)
    down_w = jnp.concatenate([v for u in down_all for v in u], axis=0)

    forget_all = small[:, :head_total]
    gain_cols = small[:, head_total:].astype(F32)
    forget_w = lax.dynamic_slice_in_dim(forget_all, at_y * heads, heads, 1)
    forget_b = lax.dynamic_slice_in_dim(forget_bias, at_y * heads, heads, 0)
    query_gain = lax.dynamic_slice_in_dim(gain_cols[:, 1], at_y * part, part).reshape(heads, head_width)
    key_gain = lax.dynamic_slice_in_dim(gain_cols[:, 2], at_y * part, part).reshape(heads, head_width)

    def split_heads(value):
        return value.reshape(4, row_count, heads, head_width)

    def join_heads(value):
        return value.reshape(4 * row_count, part)

    def scores_of(query_n, key_n, decay, allowed):
        scores = (
            jnp.einsum("bihd,bjhd->bhij", query_n, key_n, preferred_element_type=F32) / score_root
        )
        scores = scores + decay[:, :, :, None] - decay[:, :, None, :]
        return jnp.where(allowed[:, None], scores, -1e30)

    kept = []
    for m in range(micro_count):
        k = {}
        doc_ids = jnp.stack([d[m] for d in docs_all])
        allowed = (doc_ids[:, :, None] == doc_ids[:, None, :]) & (
            positions[None, None, :] <= positions[None, :, None]
        )
        group_rows = jnp.concatenate([v[m] for v in rows_y]).astype(F32)
        hidden_one = (group_rows * rms_scale(group_rows) * gain_cols[:, 0]).astype(BF16)
        mixed = product(hidden_one, attn_w)
        queries = split_heads(mixed[:, :part])
        keys_raw = split_heads(mixed[:, part : 2 * part])
        values_low = split_heads(mixed[:, 2 * part : 3 * part].astype(BF16))
        gate_pre = mixed[:, 3 * part :]
        forget_pre = (product(hidden_one, forget_w) + forget_b).reshape(4, row_count, heads)
        query_scale = rms_scale(queries)
        query_hat = queries * query_scale
        query_n = (query_hat * query_gain).astype(BF16)
        key_scale = rms_scale(keys_raw)
        key_hat = keys_raw * key_scale
        key_n = (key_hat * key_gain).astype(BF16)
        decay = jnp.cumsum(jax.nn.log_sigmoid(forget_pre), axis=1).transpose(0, 2, 1)
        scores = scores_of(query_n, key_n, decay, allowed)
        row_max = jnp.max(scores, axis=-1, keepdims=True)
        shifted = jnp.exp(scores - row_max)
        row_total = jnp.sum(shifted, axis=-1, keepdims=True)
        log_total = row_max + jnp.log(row_total)
        probs_low = (shifted / row_total).astype(BF16)
        attended = join_heads(
            jnp.einsum("bhij,bjhd->bihd", probs_low, values_low, preferred_element_type=F32)
        )
        gate_sig = jax.nn.sigmoid(gate_pre)
        gated = (attended * gate_sig).astype(BF16)
        partial = product(gated, out_w).reshape(4, row_count, width)
        rows_own = inputs[m].astype(F32)
        middle = rows_own + group_sum([partial[i] for i in range(4)], place.over_y)
        scale_two = rms_scale(middle)
        normed_two = middle * scale_two
        hidden_own = (normed_two * gain_cols[:, 3]).astype(BF16)
        hidden_two = jnp.concatenate(group_gather(hidden_own, place.over_x))
        acts = product(hidden_two, ffn_w)
        gate_act, up_act = acts[:, :hidden], acts[:, hidden:]
        gate_sg = jax.nn.sigmoid(gate_act)
        activated = (gate_act * gate_sg * up_act).astype(BF16)
        down_in = jnp.concatenate([v[m] for v in dy_x])
        partial = product(activated, down_w).reshape(4, row_count, width)
        k["result"] = (middle + group_sum([partial[i] for i in range(4)], place.over_x)).astype(BF16)
        grad_act = product_nt(down_in, down_w)
        grad_gate = (grad_act * up_act * gate_sg * (1.0 + gate_act * (1.0 - gate_sg))).astype(BF16)
        grad_upact = (grad_act * gate_act * gate_sg).astype(BF16)
        grad_both = jnp.concatenate([grad_gate, grad_upact], axis=1)
        partial = product_nt(grad_both, ffn_w).reshape(4, row_count, width)
        grad_hidden_two = group_sum([partial[i] for i in range(4)], place.over_x)
        upstream = out_grad[m].astype(F32)
        k["gain_three"] = jnp.sum(grad_hidden_two * normed_two, axis=0)
        grad_middle = upstream + norm_back(grad_hidden_two * gain_cols[:, 3], normed_two, scale_two)
        output_in = jnp.concatenate(group_gather(grad_middle.astype(BF16), place.over_y))
        k["ffn"] = (activated, down_in, hidden_two, grad_both)
        grad_gated = product_nt(output_in, out_w)
        grad_attended = split_heads((grad_gated * gate_sig).astype(BF16))
        grad_gatepre = (grad_gated * attended * gate_sig * (1.0 - gate_sig)).astype(BF16)
        probs = jnp.exp(scores_of(query_n, key_n, decay, allowed) - log_total)
        grad_probs = jnp.einsum("bihd,bjhd->bhij", grad_attended, values_low, preferred_element_type=F32)
        grad_values = jnp.einsum(
            "bhij,bihd->bjhd", probs.astype(BF16), grad_attended, preferred_element_type=F32
        )
        grad_scores = (
            probs * (grad_probs - jnp.sum(probs * grad_probs, axis=-1, keepdims=True))
        ).astype(BF16)
        grad_query_n = (
            jnp.einsum("bhij,bjhd->bihd", grad_scores, key_n, preferred_element_type=F32) / score_root
        )
        grad_key_n = (
            jnp.einsum("bhij,bihd->bjhd", grad_scores, query_n, preferred_element_type=F32) / score_root
        )
        scores_wide = grad_scores.astype(F32)
        grad_decay = (jnp.sum(scores_wide, axis=3) - jnp.sum(scores_wide, axis=2)).transpose(0, 2, 1)
        grad_logf = jnp.flip(jnp.cumsum(jnp.flip(grad_decay, 1), axis=1), 1)
        grad_forget = (
            (grad_logf * (1.0 - jax.nn.sigmoid(forget_pre))).astype(BF16).reshape(4 * row_count, heads)
        )
        k["bias"] = jnp.sum(grad_forget.astype(F32), axis=0)
        k["gain_query"] = jnp.sum(grad_query_n * query_hat, axis=(0, 1)).reshape(part)
        k["gain_key"] = jnp.sum(grad_key_n * key_hat, axis=(0, 1)).reshape(part)
        grad_query = join_heads(
            norm_back(grad_query_n * query_gain, query_hat, query_scale).astype(BF16)
        )
        grad_key = join_heads(norm_back(grad_key_n * key_gain, key_hat, key_scale).astype(BF16))
        grad_value = join_heads(grad_values.astype(BF16))
        grad_mixed = jnp.concatenate([grad_query, grad_key, grad_value, grad_gatepre], axis=1)
        partial = (product_nt(grad_mixed, attn_w) + product_nt(grad_forget, forget_w)).reshape(
            4, row_count, width
        )
        grad_hidden_one = group_sum([partial[i] for i in range(4)], place.over_y)
        scale_one = rms_scale(rows_own)
        normed_one = rows_own * scale_one
        k["gain_one"] = jnp.sum(grad_hidden_one * normed_one, axis=0)
        k["rows"] = (
            grad_middle + norm_back(grad_hidden_one * gain_cols[:, 0], normed_one, scale_one)
        ).astype(BF16)
        k["attn"] = (hidden_one, grad_mixed, grad_forget, gated, output_in)
        kept.append(k)

    def joined(name, item):
        return jnp.concatenate([k[name][item] for k in kept])

    def total_of(name):
        return sum(k[name] for k in kept)

    grad_down = product_tn(joined("ffn", 0), joined("ffn", 1)).reshape(zs, 2, -1, width)
    down_share = unit_sum(grad_down, place.over_y, y_at)
    grad_ffn = product_tn(joined("ffn", 2), joined("ffn", 3))
    grad_ffn = grad_ffn.reshape(2, 2, zs, 2, own_rows, 2 * hidden).transpose(2, 3, 0, 1, 4, 5)
    ffn_sum = unit_sum(grad_ffn, place.over_y, y_at).reshape(4, own_rows, 2 * hidden)
    grad_out = product_tn(joined("attn", 3), joined("attn", 4)).reshape(zs, 2, own_rows, width)
    out_share = send(unit_sum(grad_out, place.over_x, x_at).astype(BF16), place.swap_xy).astype(F32)
    hidden_one_all = joined("attn", 0)
    grad_attn = product_tn(hidden_one_all, joined("attn", 1))
    grad_attn = grad_attn.reshape(2, 2, zs, 2, own_rows, 4 * part).transpose(2, 0, 3, 1, 4, 5)
    attn_sum = unit_sum(grad_attn, place.over_x, x_at).reshape(4, own_rows, 4 * part)

    ffn_low = ffn_sum.astype(BF16)
    ffn_share = exchange(
        lambda j: lax.dynamic_index_in_dim(ffn_low, j, 0, keepdims=False), at_x, x_perms
    )
    attn_low = attn_sum.astype(BF16)
    attn_share = exchange(
        lambda j: lax.dynamic_index_in_dim(attn_low, j, 0, keepdims=False), at_y, y_perms
    )

    def columns(shares, first, size):
        return jnp.concatenate([s[:, first : first + size] for s in shares], axis=1).astype(F32)

    grad_forgetw = product_tn(hidden_one_all, joined("attn", 2))
    small_grad = jnp.zeros((width, head_total + 4), F32)
    small_grad = lax.dynamic_update_slice(small_grad, grad_forgetw, (0, at_y * heads))
    zero = jnp.zeros((width,), F32)
    gain_grad = jnp.stack(
        [
            total_of("gain_one"),
            lax.dynamic_update_slice(zero, total_of("gain_query"), (at_y * part,)),
            lax.dynamic_update_slice(zero, total_of("gain_key"), (at_y * part,)),
            total_of("gain_three"),
        ],
        axis=1,
    )
    small_grad = small_grad.at[:, head_total:].set(gain_grad)
    small_share = lax.psum_scatter(small_grad, BOTH, scatter_dimension=0, tiled=True)
    bias_sum = lax.psum(
        lax.dynamic_update_slice(jnp.zeros((head_total,), F32), total_of("bias"), (at_y * heads,)),
        BOTH,
    )
    return (
        jnp.stack([k["result"] for k in kept]),
        jnp.stack([k["rows"] for k in kept]),
        columns(attn_share, 0, part),
        columns(attn_share, part, part),
        columns(attn_share, 2 * part, part),
        columns(attn_share, 3 * part, part),
        out_share,
        small_share[:, :head_total],
        bias_sum,
        small_share[:, head_total:],
        columns(ffn_share, 0, hidden),
        columns(ffn_share, hidden, hidden),
        down_share,
    )


def solution(mesh):
    place = Place(mesh)
    rows = P(BOTH, None)
    tokens = P(None, BOTH, None)
    in_specs = (tokens,) * 3 + (rows,) * 6 + (P(),) + (rows,) * 4
    out_specs = (tokens,) * 2 + (rows,) * 6 + (P(),) + (rows,) * 4

    def step(*args):
        return local(place, *args)

    return jax.shard_map(step, mesh=mesh, in_specs=in_specs, out_specs=out_specs, check_vma=False)
```

time: 2460 us -> 1010 us (0.41)
  waiting for transfers between devices: 1880 us -> 343 us
  matrix products: 313 us -> 119 us
  starting transfers between devices: 1.51 us -> 181 us
  other arithmetic: 20 us -> 115 us
  blocking collectives: 174 us -> 105 us
  local copies, waits for them, and re-layouts: 42 us -> 109 us
    reduce_scatter x8 -> x0, waiting for transfers between devices: 1460 us -> none  [the longest x1 253 us: spread(): lax.psum_scatter(down_g, ('dp', 'fsdp'), scatter_dimension=0, tiled=True)]
    all_gather x8 -> x0, waiting for transfers between devices: 407 us -> none  [the longest x1 90.6 us: collect(): lax.all_gather(up_w, ('dp', 'fsdp'), axis=0, tiled=True)]
    ppermute x0 -> x139, waiting for transfers between devices: none -> 274 us  [send(): return lax.ppermute(value, BOTH, perm)]
    ppermute x0 -> x139, starting transfers between devices: none -> 181 us  [send(): return lax.ppermute(value, BOTH, perm)]
    dot_general x18 -> x5, matrix products: 128 us -> 30.4 us  [product_tn(): lax.dot_general(left_side, right_side, (((0,), (0,)), ((), ())), preferre...]
    all_gather x2 -> x1, blocking collectives: 135 us -> 67.9 us  [local(): lax.all_gather(jnp.concatenate([forget_weight, gains], axis=1), BOTH, axi...]
    unnamed x20 -> x2, waiting for transfers between devices: 14 us -> 68.6 us
    dot_general x30 -> x22, matrix products: 91.9 us -> 43.7 us  [the longest x10 22.7 us: product(): return jnp.dot(left_side, right_side, preferred_element_type=F32)]
  transfers between devices with their start and end apart: 18 -> 140, of which waited for: 15 -> 43; matrix products, arithmetic and copies ran while one was open for 9% -> 30% of each run, Pallas kernels for 0% -> 0%
where the time goes in v1:
time: 1010 us; the launch traced here: 992 us
  waiting for transfers between devices  343 us (34%)
  starting transfers between devices  181 us (18%)
  matrix products  119 us (12%)
  other arithmetic  115 us (11%)
  local copies, waits for them, and re-layouts  109 us (11%)
  blocking collectives  105 us (10%)
  between operations  19.8 us (2%)
    ppermute x139, waiting for transfers between devices, send(): return lax.ppermute(value, BOTH, perm)  274 us
    ppermute x139, starting transfers between devices, send(): return lax.ppermute(value, BOTH, perm)  181 us
    unnamed x2, waiting for transfers between devices  68.6 us
    all_gather x1, blocking collectives, local(): lax.all_gather(jnp.concatenate([forget_weight, gains], axis=1), BOTH, axi...  67.9 us
    dot_general x10, matrix products, product_nt(): lax.dot_general(left_side, right_side, (((1,), (1,)), ((), ())), preferre...  45 us
    unnamed x433, local copies, waits for them, and re-layouts  38.5 us
    psum x1, blocking collectives, local(): lax.psum(lax.dynamic_update_slice(jnp.zeros((head_total,), F32), total_of...  37.1 us
    convert_element_type x16, other arithmetic, unit_sum(): carried = send(term.astype(BF16), place.toward(sign, offset)).astype(F32)  32.8 us
  transfers between devices with their start and end apart: 140, of which 43 were waited for; matrix products, arithmetic and copies ran while one was open for 30% of the time, Pallas kernels for 0%

profile of v1, /device:TPU:0, one launch (start us, length us, event | category | flops | bytes accessed | tf_op | source)
XLA Modules:
  0.0 991.9 jit_solution(17541783668141938140)
XLA Ops:
  27.4 67.9 %all-gather = bf16[32,48,28]{1,2,0:T(8,128)(2,1)S(1)} all-gather(bf16[1,48,28]{1,2,0:T(8,128)(2,1)S(1)} %maximum_bitcast_fusion.1), channel_id=1, replica_groups=mesh['dp'=4,'fsdp'=8] {'dp','fsdp'}, dimensions={0}, use_global_device_ids=true | all-gather | bytes 88704 | tf_op jit(solution)/shard_map/all_gather | solution.py:201
  129.0 9.4 collective-permute-done.26
  156.8 13.8 %collective-permute-done.71 = bf16[2,128,1536]{2,1,0:T(8,128)(2,1)} collective-permute-done((bf16[2,128,1536]{2,1,0:T(8,128)(2,1)S(1)}, bf16[2,128,1536]{2,1,0:T(8,128)(2,1)}, u32[]{:S(2)}, u32[]{:S(2)}) %collective-permute-start.71) | collective-permute-done | bytes 786464 | tf_op jit(solution)/shard_map/ppermute | solution.py:89
  174.9 10.9 %collective-permute-done = bf16[2,128,1536]{2,1,0:T(8,128)(2,1)S(1)} collective-permute-done((bf16[2,128,1536]{2,1,0:T(8,128)(2,1)S(1)}, bf16[2,128,1536]{2,1,0:T(8,128)(2,1)S(1)}, u32[]{:S(2)}, u32[]{:S(2)}) %collective-permute-start) | collective-permute-done | bytes 786464 | tf_op jit(solution)/shard_map/ppermute | solution.py:89
  197.7 16.6 %collective-permute-done.55 = bf16[128,1536]{1,0:T(8,128)(2,1)S(1)} collective-permute-done((bf16[128,1536]{1,0:T(8,128)(2,1)S(1)}, bf16[128,1536]{1,0:T(8,128)(2,1)S(1)}, u32[]{:S(2)}, u32[]{:S(2)}) %collective-permute-start.55) | collective-permute-done | bytes 393248 | tf_op jit(solution)/shard_map/ppermute | solution.py:89
  218.2 10.9 %collective-permute-done.56 = bf16[128,1536]{1,0:T(8,128)(2,1)S(1)} collective-permute-done((bf16[128,1536]{1,0:T(8,128)(2,1)S(1)}, bf16[128,1536]{1,0:T(8,128)(2,1)S(1)}, u32[]{:S(2)}, u32[]{:S(2)}) %collective-permute-start.56) | collective-permute-done | bytes 393248 | tf_op jit(solution)/shard_map/ppermute | solution.py:89
  299.7 14.6 %collective-permute-done.46 = bf16[4,48,2048]{2,1,0:T(8,128)(2,1)S(1)} collective-permute-done((bf16[4,48,2048]{2,1,0:T(8,128)(2,1)S(1)}, bf16[4,48,2048]{2,1,0:T(8,128)(2,1)S(1)}, u32[]{:S(2)}, u32[]{:S(2)}) %collective-permute-start.46) | collective-permute-done | bytes 786464 | tf_op jit(solution)/shard_map/ppermute | solution.py:89
  370.5 22.9 %collective-permute-done.32 = bf16[128,1536]{1,0:T(8,128)(2,1)S(1)} collective-permute-done((bf16[128,1536]{1,0:T(8,128)(2,1)S(1)}, bf16[128,1536]{1,0:T(8,128)(2,1)S(1)}, u32[]{:S(2)}, u32[]{:S(2)}) %collective-permute-start.32) | collective-permute-done | bytes 393248 | tf_op jit(solution)/shard_map/ppermute | solution.py:89
  393.4 7.6 collective-permute-done.64
  406.6 7.6 collective-permute-done.33
  434.8 7.5 collective-permute-done.76
  442.3 8.0 collective-permute-done.61
  509.4 11.6 %fusion = f32[1536,2048]{1,0:T(8,128)S(1)} fusion(bf16[1024,1536]{1,0:T(8,128)(2,1)} %constant_dynamic-update-slice_fusion.8, bf16[512,1024]{1,0:T(8,128)(2,1)} %copy-done.192, bf16[512,1024]{1,0:T(8,128)(2,1)} %copy-done.191, bf16[512,1024]{1,0:T(8,128)(2,1)} %copy-done.190, bf16[512,1024]{1,0:T(8,128)(2,1)S(1)} %copy-done.189), kind=kOutput, calls=%fused_computation.2 | convolution fusion | flops 6459228160 | bytes 19922944 | tf_op jit(solution)/shard_map/dot_general | solution.py:28
  537.2 8.0 collective-permute-done.70
  563.1 22.1 %collective-permute-done.86 = bf16[128,1536]{1,0:T(8,128)(2,1)S(1)} collective-permute-done((bf16[128,1536]{1,0:T(8,128)(2,1)S(1)}, bf16[128,1536]{1,0:T(8,128)(2,1)S(1)}, u32[]{:S(2)}, u32[]{:S(2)}) %collective-permute-start.86) | collective-permute-done | bytes 393248 | tf_op jit(solution)/shard_map/ppermute | solution.py:89
  585.8 7.9 collective-permute-done.132
  634.7 6.9 fusion.77
  648.6 9.3 fusion.14
  684.1 8.9 collective-permute-done.120
  713.8 37.1 %psum.7 = f32[24]{0:T(128)} all-reduce(f32[24]{0:T(128)} %add_dynamic-update-slice_fusion), channel_id=1, replica_groups=mesh['dp'=4,'fsdp'=8] {'dp','fsdp'}, use_global_device_ids=true, to_apply=%region_43.44 | all-reduce | flops 24 | bytes 192 | tf_op jit(solution)/shard_map/psum | solution.py:412
  773.9 7.0 collective-permute-start.110
  803.6 7.4 collective-permute-done.95
  861.8 68.6 %reduce-scatter.4.cloned.1.call-done = f32[48,28]{1,0:T(8,128)} async-done(((f32[1536,28]{1,0:T(8,128)}), f32[48,28]{1,0:T(8,128)}) %reduce-scatter.4.cloned.1.call-update) | async-done | bytes 5392
  962.7 7.0 collective-permute-done.98
  (992 shorter events, 572.7 us)
Async XLA Ops:
  7.2 923.2 %reduce-scatter.4.cloned.1.call-start = ((), (), s32[]{:S(2)}) async-start(), calls=%async_computation.1 | async-start | bytes 811008
  7.2 96.0 %collective-permute-start.16 = (s32[2,1,128]{2,1,0:T(1,128)}, s32[2,1,128]{2,1,0:T(1,128)}, u32[]{:S(2)}, u32[]{:S(2)}) collective-permute-start(s32[2,1,128]{2,1,0:T(1,128)} %param.33), channel_id=1, source_target_pairs={{0,1},{1,0},{2,3},{3,2},{4,5},{5,4},{6,7},{7,6},{8,9},{9,8},{10,11... | collective-permute-start | bytes 3080 | tf_op jit(solution)/shard_map/ppermute | solution.py:89
  10.3 93.6 %collective-permute-start.17 = (s32[2,1,128]{2,1,0:T(1,128)}, s32[2,1,128]{2,1,0:T(1,128)}, u32[]{:S(2)}, u32[]{:S(2)}) collective-permute-start(s32[2,1,128]{2,1,0:T(1,128)} %param.33), channel_id=1, source_target_pairs={{0,8},{1,9},{2,10},{3,11},{4,12},{5,13},{6,14},{7,15},{8,0},{9,1},... | collective-permute-start | bytes 3080 | tf_op jit(solution)/shard_map/ppermute | solution.py:89
  10.3 99.6 %collective-permute-start.19 = (bf16[48,1536]{1,0:T(8,128)(2,1)}, bf16[48,1536]{1,0:T(8,128)(2,1)S(1)}, u32[]{:S(2)}, u32[]{:S(2)}) collective-permute-start(bf16[48,1536]{1,0:T(8,128)(2,1)} %param.39), channel_id=1, source_target_pairs={{0,0},{1,16},{2,2},{3,18},{4,4},{5,20},{6,6},{7,22},{8,8},{9,24},{... | collective-permute-start | bytes 442376 | tf_op jit(solution)/shard_map/ppermute | solution.py:89
  16.4 93.5 %collective-permute-start.4 = (bf16[48,1536]{1,0:T(8,128)(2,1)}, bf16[48,1536]{1,0:T(8,128)(2,1)}, u32[]{:S(2)}, u32[]{:S(2)}) collective-permute-start(bf16[48,1536]{1,0:T(8,128)(2,1)} %get-tuple-element.255), channel_id=1, source_target_pairs={{0,1},{1,0},{2,3},{3,2},{4,5},{5,4},{6,7},{7,6},{8,9},{9,8},{10,11... | collective-permute-start | bytes 442376 | tf_op jit(solution)/shard_map/ppermute | solution.py:89
  19.7 90.3 %collective-permute-start.5 = (bf16[48,1536]{1,0:T(8,128)(2,1)}, bf16[48,1536]{1,0:T(8,128)(2,1)}, u32[]{:S(2)}, u32[]{:S(2)}) collective-permute-start(bf16[48,1536]{1,0:T(8,128)(2,1)} %get-tuple-element.256), channel_id=1, source_target_pairs={{0,9},{1,8},{2,11},{3,10},{4,13},{5,12},{6,15},{7,14},{8,1},{9,0},... | collective-permute-start | bytes 442376 | tf_op jit(solution)/shard_map/ppermute | solution.py:89
  150.5 86.6 %collective-permute-start.52 = (bf16[128,1536]{1,0:T(8,128)(2,1)S(1)}, bf16[128,1536]{1,0:T(8,128)(2,1)S(1)}, u32[]{:S(2)}, u32[]{:S(2)}) collective-permute-start(bf16[128,1536]{1,0:T(8,128)(2,1)S(1)} %copy-done.37), channel_id=1, source_target_pairs={{0,1},{1,0},{2,3},{3,2},{4,5},{5,4},{6,7},{7,6},{8,9},{9,8},{10,11... | collective-permute-start | bytes 1179656 | tf_op jit(solution)/shard_map/ppermute | solution.py:89
  214.2 76.5 %collective-permute-start.9 = (bf16[4,48,1536]{2,1,0:T(8,128)(2,1)}, bf16[4,48,1536]{2,1,0:T(8,128)(2,1)}, u32[]{:S(2)}, u32[]{:S(2)}) collective-permute-start(bf16[4,48,1536]{2,1,0:T(8,128)(2,1)} %pad_maximum_fusion.8), channel_id=1, source_target_pairs={{0,16},{1,17},{2,18},{3,19},{4,20},{5,21},{6,22},{7,23},{8,24},{9,... | collective-permute-start | bytes 1769480 | tf_op jit(solution)/shard_map/ppermute | solution.py:89
  229.1 62.3 %collective-permute-start.11 = (bf16[4,48,1536]{2,1,0:T(8,128)(2,1)}, bf16[4,48,1536]{2,1,0:T(8,128)(2,1)}, u32[]{:S(2)}, u32[]{:S(2)}) collective-permute-start(bf16[4,48,1536]{2,1,0:T(8,128)(2,1)} %select_select_fusion.22), channel_id=1, source_target_pairs={{0,16},{1,17},{2,18},{3,19},{4,20},{5,21},{6,22},{7,23},{8,24},{9,... | collective-permute-start | bytes 1769480 | tf_op jit(solution)/shard_map/ppermute | solution.py:89
  290.8 71.4 %collective-permute-start.42 = (bf16[4,48,2048]{2,1,0:T(8,128)(2,1)}, bf16[4,48,2048]{2,1,0:T(8,128)(2,1)}, u32[]{:S(2)}, u32[]{:S(2)}) collective-permute-start(bf16[4,48,2048]{2,1,0:T(8,128)(2,1)} %copy-done.105), channel_id=1, source_target_pairs={{0,1},{1,0},{2,3},{3,2},{4,5},{5,4},{6,7},{7,6},{8,9},{9,8},{10,11... | collective-permute-start | bytes 2359304 | tf_op jit(solution)/shard_map/ppermute | solution.py:89
  291.4 70.9 %collective-permute-start.44 = (bf16[4,48,2048]{2,1,0:T(8,128)(2,1)}, bf16[4,48,2048]{2,1,0:T(8,128)(2,1)}, u32[]{:S(2)}, u32[]{:S(2)}) collective-permute-start(bf16[4,48,2048]{2,1,0:T(8,128)(2,1)} %select_select_fusion.13), channel_id=1, source_target_pairs={{0,1},{1,0},{2,3},{3,2},{4,5},{5,4},{6,7},{7,6},{8,9},{9,8},{10,11... | collective-permute-start | bytes 2359304 | tf_op jit(solution)/shard_map/ppermute | solution.py:89
  530.8 151.3 %collective-permute-start.118 = (bf16[2,2,48,2048]{3,2,1,0:T(8,128)(2,1)}, bf16[2,2,48,2048]{3,2,1,0:T(8,128)(2,1)}, u32[]{:S(2)}, u32[]{:S(2)}) collective-permute-start(bf16[2,2,48,2048]{3,2,1,0:T(8,128)(2,1)} %get-tuple-element.134), channel_id=1, source_target_pairs={{0,1},{1,0},{2,3},{3,2},{4,5},{5,4},{6,7},{7,6},{8,9},{9,8},{10,11... | collective-permute-start | bytes 2359304 | tf_op jit(solution)/shard_map/ppermute | solution.py:89
  585.3 88.8 %collective-permute-start.131 = (bf16[128,1536]{1,0:T(8,128)(2,1)}, bf16[128,1536]{1,0:T(8,128)(2,1)}, u32[]{:S(2)}, u32[]{:S(2)}) collective-permute-start(bf16[128,1536]{1,0:T(8,128)(2,1)} %get-tuple-element.149), channel_id=1, source_target_pairs={{0,1},{1,0},{2,3},{3,2},{4,5},{5,4},{6,7},{7,6},{8,9},{9,8},{10,11... | collective-permute-start | bytes 1179656 | tf_op jit(solution)/shard_map/ppermute | solution.py:89
  593.7 89.5 %collective-permute-start.123 = (bf16[2,2,48,2048]{3,2,1,0:T(8,128)(2,1)}, bf16[2,2,48,2048]{3,2,1,0:T(8,128)(2,1)}, u32[]{:S(2)}, u32[]{:S(2)}) collective-permute-start(bf16[2,2,48,2048]{3,2,1,0:T(8,128)(2,1)} %fusion.44), channel_id=1, source_target_pairs={{6,4},{7,5},{14,12},{15,13},{22,20},{23,21},{30,28},{31,29}} | collective-permute-start | bytes 2359304 | tf_op jit(solution)/shard_map/ppermute | solution.py:89
  605.6 71.9 %collective-permute-start.136 = (bf16[128,1536]{1,0:T(8,128)(2,1)}, bf16[128,1536]{1,0:T(8,128)(2,1)}, u32[]{:S(2)}, u32[]{:S(2)}) collective-permute-start(bf16[128,1536]{1,0:T(8,128)(2,1)} %fusion.144), channel_id=1, source_target_pairs={{6,4},{7,5},{14,12},{15,13},{22,20},{23,21},{30,28},{31,29}} | collective-permute-start | bytes 1179656 | tf_op jit(solution)/shard_map/ppermute | solution.py:89
  607.9 70.3 %collective-permute-start.133 = (bf16[128,1536]{1,0:T(8,128)(2,1)}, bf16[128,1536]{1,0:T(8,128)(2,1)}, u32[]{:S(2)}, u32[]{:S(2)}) collective-permute-start(bf16[128,1536]{1,0:T(8,128)(2,1)} %get-tuple-element.51), channel_id=1, source_target_pairs={{0,2},{1,3},{8,10},{9,11},{16,18},{17,19},{24,26},{25,27}} | collective-permute-start | bytes 1179656 | tf_op jit(solution)/shard_map/ppermute | solution.py:89
  677.6 90.6 %collective-permute-start.130 = (bf16[128,1536]{1,0:T(8,128)(2,1)}, bf16[128,1536]{1,0:T(8,128)(2,1)}, u32[]{:S(2)}, u32[]{:S(2)}) collective-permute-start(bf16[128,1536]{1,0:T(8,128)(2,1)} %get-tuple-element.147), channel_id=1, source_target_pairs={{0,1},{1,0},{2,3},{3,2},{4,5},{5,4},{6,7},{7,6},{8,9},{9,8},{10,11... | collective-permute-start | bytes 1179656 | tf_op jit(solution)/shard_map/ppermute | solution.py:89
  678.2 106.6 %collective-permute-start.106 = (bf16[48,1536]{1,0:T(8,128)(2,1)}, bf16[48,1536]{1,0:T(8,128)(2,1)}, u32[]{:S(2)}, u32[]{:S(2)}) collective-permute-start(bf16[48,1536]{1,0:T(8,128)(2,1)} %get-tuple-element.179), channel_id=1, source_target_pairs={{0,16},{1,17},{2,18},{3,19},{4,20},{5,21},{6,22},{7,23},{8,24},{9,... | collective-permute-start | bytes 442376 | tf_op jit(solution)/shard_map/ppermute | solution.py:89
  683.2 77.9 %collective-permute-start.107 = (bf16[48,1536]{1,0:T(8,128)(2,1)}, bf16[48,1536]{1,0:T(8,128)(2,1)S(1)}, u32[]{:S(2)}, u32[]{:S(2)}) collective-permute-start(bf16[48,1536]{1,0:T(8,128)(2,1)} %get-tuple-element.181), channel_id=1, source_target_pairs={{0,16},{1,17},{2,18},{3,19},{4,20},{5,21},{6,22},{7,23},{8,24},{9,... | collective-permute-start | bytes 442376 | tf_op jit(solution)/shard_map/ppermute | solution.py:89
  821.4 111.8 %collective-permute-start.94 = (bf16[2,2,48,1536]{3,2,1,0:T(8,128)(2,1)}, bf16[2,2,48,1536]{3,2,1,0:T(8,128)(2,1)}, u32[]{:S(2)}, u32[]{:S(2)}) collective-permute-start(bf16[2,2,48,1536]{3,2,1,0:T(8,128)(2,1)} %bitcast.631), channel_id=1, source_target_pairs={{0,16},{1,17},{2,18},{3,19},{4,20},{5,21},{6,22},{7,23},{8,24},{9,... | collective-permute-start | bytes 1769480 | tf_op jit(solution)/shard_map/ppermute | solution.py:89
  842.5 92.2 %collective-permute-start.99 = (bf16[2,2,48,1536]{3,2,1,0:T(8,128)(2,1)}, bf16[2,2,48,1536]{3,2,1,0:T(8,128)(2,1)}, u32[]{:S(2)}, u32[]{:S(2)}) collective-permute-start(bf16[2,2,48,1536]{3,2,1,0:T(8,128)(2,1)} %fusion.116), channel_id=1, source_target_pairs={{6,4},{7,5},{14,12},{15,13},{22,20},{23,21},{30,28},{31,29}} | collective-permute-start | bytes 1769480 | tf_op jit(solution)/shard_map/ppermute | solution.py:89
  844.0 90.7 %collective-permute-start.96 = (bf16[2,2,48,1536]{3,2,1,0:T(8,128)(2,1)}, bf16[2,2,48,1536]{3,2,1,0:T(8,128)(2,1)}, u32[]{:S(2)}, u32[]{:S(2)}) collective-permute-start(bf16[2,2,48,1536]{3,2,1,0:T(8,128)(2,1)} %get-tuple-element.71), channel_id=1, source_target_pairs={{0,2},{1,3},{8,10},{9,11},{16,18},{17,19},{24,26},{25,27}} | collective-permute-start | bytes 1769480 | tf_op jit(solution)/shard_map/ppermute | solution.py:89
  855.3 86.5 %collective-permute-start.122 = (bf16[2,2,48,2048]{3,2,1,0:T(8,128)(2,1)}, bf16[2,2,48,2048]{3,2,1,0:T(8,128)(2,1)}, u32[]{:S(2)}, u32[]{:S(2)}) collective-permute-start(bf16[2,2,48,2048]{3,2,1,0:T(8,128)(2,1)} %get-tuple-element.127), channel_id=1, source_target_pairs={{0,2},{1,3},{2,4},{3,5},{4,6},{5,7},{8,10},{9,11},{10,12},{11,13},... | collective-permute-start | bytes 2359304 | tf_op jit(solution)/shard_map/ppermute | solution.py:89
  857.5 84.3 %collective-permute-start.125 = (bf16[2,2,48,2048]{3,2,1,0:T(8,128)(2,1)}, bf16[2,2,48,2048]{3,2,1,0:T(8,128)(2,1)}, u32[]{:S(2)}, u32[]{:S(2)}) collective-permute-start(bf16[2,2,48,2048]{3,2,1,0:T(8,128)(2,1)} %get-tuple-element.128), channel_id=1, source_target_pairs={{2,0},{3,1},{4,2},{5,3},{6,4},{7,5},{10,8},{11,9},{12,10},{13,11},... | collective-permute-start | bytes 2359304 | tf_op jit(solution)/shard_map/ppermute | solution.py:89
  (314 other events, 4724.0 us)
Sparse Core Ops, SparseCore 0:
  835.8 94.5 reduce-scatter.3
